TPU v7x, 256 devices: a whole 4x4x8 slice. The times are simulated.
256 devices in a mesh: row: 32 (over y_lo, z, core), col: 8 (over x, y_hi).
Axes of the slice: x: 4, y: 4 (y_hi: 2, y_lo: 2; y = y_hi * 2 + y_lo), z: 8, core: 2. Of those that a mesh axis runs over, the one named last changes fastest.
Arguments:
- start_block: float32 [32768, 256], P(('row', 'col')), may hold values from -6 to 6
- tiles: bfloat16 [32, 8, 14, 128, 128], P('row', 'col'), may hold values from -0.125 to 0.125
- tile_rows: int32 [32, 8, 14], P('row', 'col'), may hold values from -1 to 255, as said below
- tile_cols: int32 [32, 8, 14], P('row', 'col'), may hold values from -1 to 255, as said below
- bounds: float32 [3], replicated, may hold values from -2.6 to 2.6, as said below
Outputs:
- filtered: float32 [32768, 256], P(('row', 'col'))
Inputs may be any that keep to these rules, and one draw needn't show every extreme that they name: Vector rows form blocks of 128 rows, one block a device, in row+col order. On the device at grid row r and grid column c, a live slot names a block row held by one of the devices (r, any column) and a block column held by one of the devices (any row, c). Live slots come first; each device has 1 to 14 live slots, and one device has exactly 14 in every draw. No block position is named twice, and the mirror of a named position is never named unless it lies on the diagonal. tile_rows and tile_cols are -1 together. `tile_cols`: same slots as tile_rows. bounds[0] < bounds[1] < bounds[2].
All inputs are finite; a program needn't handle non-finite values.
Results may differ from a plain program's by a relative error of at most 0.0042.
Values may be sent and summed in bfloat16 or wider, within the bound.
No kernel may reach another device: no remote copies, remote signals or barrier semaphores. Data moves between devices by JAX's collectives and lax.ppermute only.
A program may use at most 64 MiB of HBM per device.

v0:
```python
import jax
import jax.numpy as jnp
from jax import lax
from jax.sharding import PartitionSpec as P

DEGREE = 4


def local(start_block, tiles, tile_rows, tile_cols, bounds):
    rows_dev, vec_width = start_block.shape
    tile_size = tiles.shape[-1]
    blocks = rows_dev // tile_size
    row_count = lax.axis_size("row")
    col_count = lax.axis_size("col")
    near_count = col_count * blocks
    far_count = row_count * blocks
    row_index = lax.axis_index("row")
    slots = tiles.shape[2]
    tile_mats = tiles.reshape(slots, tile_size, tile_size)
    glob_rows = tile_rows.reshape(slots)
    glob_cols = tile_cols.reshape(slots)
    is_live = glob_rows >= 0
    local_rows = jnp.where(is_live, glob_rows - row_index * near_count, -1)
    local_cols = jnp.where(
        is_live, glob_cols // blocks // col_count * blocks + glob_cols % blocks, -1
    )
    row_table = (local_rows[None, :] == lax.iota(jnp.int32, near_count)[:, None]).astype(
        jnp.float32
    )
    col_table = (local_cols[None, :] == lax.iota(jnp.int32, far_count)[:, None]).astype(jnp.float32)
    rows_safe = jnp.maximum(local_rows, 0)
    cols_safe = jnp.maximum(local_cols, 0)

    def apply_matrix(vectors):
        low_vectors = vectors.astype(jnp.bfloat16)
        far_vectors = lax.all_gather(low_vectors, "row", axis=0, tiled=True).reshape(
            far_count, tile_size, vec_width
        )
        near_vectors = lax.all_gather(low_vectors, "col", axis=0, tiled=True).reshape(
            near_count, tile_size, vec_width
        )
        picked_far = jnp.take(far_vectors, cols_safe, axis=0)
        picked_near = jnp.take(near_vectors, rows_safe, axis=0)
        forward = jnp.einsum(
            "txy,tyk->txk", tile_mats, picked_far, preferred_element_type=jnp.float32
        )
        backward = jnp.einsum(
            "tyx,tyk->txk", tile_mats, picked_near, preferred_element_type=jnp.float32
        )
        near_partial = jnp.dot(
            row_table, forward.reshape(slots, -1), precision=lax.Precision.HIGHEST
        )
        far_partial = jnp.dot(
            col_table, backward.reshape(slots, -1), precision=lax.Precision.HIGHEST
        )
        mirrored = lax.psum_scatter(
            far_partial.reshape(far_count * tile_size, vec_width),
            "row",
            scatter_dimension=0,
            tiled=True,
        )
        combined = lax.psum_scatter(
            near_partial.reshape(near_count * tile_size, vec_width),
            "col",
            scatter_dimension=0,
            tiled=True,
        )
        return combined + mirrored

    half_width = (bounds[2] - bounds[1]) * 0.5
    center = (bounds[2] + bounds[1]) * 0.5
    sigma_one = half_width / (bounds[0] - center)
    previous = start_block
    current = (apply_matrix(start_block) - center * start_block) * (sigma_one / half_width)
    sigma = sigma_one
    for turn_index in range(DEGREE - 1):
        sigma_next = 1.0 / (2.0 / sigma_one - sigma)
        product = apply_matrix(current)
        following = (product - center * current) * (
            2.0 * sigma_next / half_width
        ) - sigma * sigma_next * previous
        previous = current
        current = following
        sigma = sigma_next
    return current


def solution(mesh):
    placed = (
        P(("row", "col"), None),
        P("row", "col", None, None, None),
        P("row", "col", None),
        P("row", "col", None),
        P(),
    )
    return jax.shard_map(
        local, mesh=mesh, in_specs=placed, out_specs=P(("row", "col"), None), check_vma=False
    )
```

profile of v0, /device:TPU:2, one launch (start us, length us, event | category | flops | bytes accessed | tf_op | source)
XLA Modules:
  0.0 1115.5 jit_solution(15374100512210820898)
XLA Ops:
  6.5 1.6 convert_element_type.14
  8.9 68.0 %all-gather.5.cloned.1.call-done = bf16[4096,256]{1,0:T(8,128)(2,1)} async-done(((bf16[128,256]{1,0:T(8,128)(2,1)}), bf16[4096,256]{1,0:T(8,128)(2,1)}) %all-gather.5.cloned.1.call-update) | async-done | bytes 2097168 | tf_op jit(solution)/shard_map/all_gather | solution.py:36
  76.9 2.2 gather_fusion
  79.6 1.7 copy.7
  81.4 1.7 pad.8
  83.1 1.2 copy.30
  84.3 0.8 fusion.43
  85.1 1.2 reshape.147
  86.5 33.2 %all_gather.25 = bf16[1024,256]{1,0:T(8,128)(2,1)S(1)} all-gather(bf16[128,256]{1,0:T(8,128)(2,1)S(1)} %copy-done.3), channel_id=1, replica_groups=mesh['row'=32,'col'=8] {'col'}, dimensions={0}, use_global_device_ids=true | all-gather | bytes 589824 | tf_op jit(solution)/shard_map/all_gather | solution.py:39
  120.8 1.7 copy.9
  122.5 1.7 pad.9
  124.2 1.2 copy.31
  125.4 3.8 fusion.35
  129.3 4.9 reshape.150
  138.5 24.8 %reduce-scatter.9.cloned.1.call-done = f32[128,256]{1,0:T(8,128)} async-done(((f32[1024,256]{1,0:T(8,128)}), f32[128,256]{1,0:T(8,128)}) %reduce-scatter.9.cloned.1.call-update) | async-done | bytes 131088 | tf_op jit(solution)/shard_map/reduce_scatter | solution.py:62
  163.3 124.4 %reduce-scatter.11.cloned.1.call-done = f32[128,256]{1,0:T(8,128)} async-done(((f32[4096,256]{1,0:T(8,128)}), f32[128,256]{1,0:T(8,128)}) %reduce-scatter.11.cloned.1.call-update) | async-done | bytes 131088 | tf_op jit(solution)/shard_map/reduce_scatter | solution.py:56
  287.7 1.6 fusion.58
  289.4 60.7 %all-gather.7.cloned.1.call-done = bf16[4096,256]{1,0:T(8,128)(2,1)} async-done(((bf16[128,256]{1,0:T(8,128)(2,1)}), bf16[4096,256]{1,0:T(8,128)(2,1)}) %all-gather.7.cloned.1.call-update) | async-done | bytes 2097168 | tf_op jit(solution)/shard_map/all_gather | solution.py:36
  350.1 2.2 gather_fusion.2
  352.8 1.7 copy.11
  354.5 1.7 pad.10
  356.3 1.2 copy.32
  357.5 0.8 fusion.42
  358.3 1.2 reshape.153
  359.6 33.3 %all_gather.27 = bf16[1024,256]{1,0:T(8,128)(2,1)S(1)} all-gather(bf16[128,256]{1,0:T(8,128)(2,1)S(1)} %copy-done.6), channel_id=1, replica_groups=mesh['row'=32,'col'=8] {'col'}, dimensions={0}, use_global_device_ids=true | all-gather | bytes 589824 | tf_op jit(solution)/shard_map/all_gather | solution.py:39
  394.1 1.7 copy.13
  395.8 1.7 pad.11
  397.5 1.2 copy.33
  398.8 3.8 fusion.34
  402.6 4.9 reshape.156
  407.7 29.0 %reduce-scatter.13.cloned.1.call-done = f32[128,256]{1,0:T(8,128)} async-done(((f32[1024,256]{1,0:T(8,128)}), f32[128,256]{1,0:T(8,128)}) %reduce-scatter.13.cloned.1.call-update) | async-done | bytes 131088 | tf_op jit(solution)/shard_map/reduce_scatter | solution.py:62
  436.6 124.1 %reduce-scatter.15.cloned.1.call-done = f32[128,256]{1,0:T(8,128)} async-done(((f32[4096,256]{1,0:T(8,128)}), f32[128,256]{1,0:T(8,128)}) %reduce-scatter.15.cloned.1.call-update) | async-done | bytes 131088 | tf_op jit(solution)/shard_map/reduce_scatter | solution.py:56
  560.7 1.6 fusion.57
  562.4 60.7 %all-gather.9.cloned.1.call-done = bf16[4096,256]{1,0:T(8,128)(2,1)} async-done(((bf16[128,256]{1,0:T(8,128)(2,1)}), bf16[4096,256]{1,0:T(8,128)(2,1)}) %all-gather.9.cloned.1.call-update) | async-done | bytes 2097168 | tf_op jit(solution)/shard_map/all_gather | solution.py:36
  623.1 2.2 gather_fusion.4
  625.8 1.7 copy.15
  627.6 1.7 pad.12
  629.3 1.2 copy.34
  630.5 0.8 fusion.41
  631.3 1.2 reshape.159
  632.6 33.5 %all_gather.29 = bf16[1024,256]{1,0:T(8,128)(2,1)S(1)} all-gather(bf16[128,256]{1,0:T(8,128)(2,1)S(1)} %copy-done.5), channel_id=1, replica_groups=mesh['row'=32,'col'=8] {'col'}, dimensions={0}, use_global_device_ids=true | all-gather | bytes 589824 | tf_op jit(solution)/shard_map/all_gather | solution.py:39
  667.3 1.7 copy.17
  669.0 1.7 pad.13
  670.7 1.2 copy.35
  672.0 3.8 fusion.33
  675.8 4.9 reshape.162
  680.8 28.9 %reduce-scatter.17.cloned.1.call-done = f32[128,256]{1,0:T(8,128)} async-done(((f32[1024,256]{1,0:T(8,128)}), f32[128,256]{1,0:T(8,128)}) %reduce-scatter.17.cloned.1.call-update) | async-done | bytes 131088 | tf_op jit(solution)/shard_map/reduce_scatter | solution.py:62
  709.7 124.3 %reduce-scatter.19.cloned.1.call-done = f32[128,256]{1,0:T(8,128)} async-done(((f32[4096,256]{1,0:T(8,128)}), f32[128,256]{1,0:T(8,128)}) %reduce-scatter.19.cloned.1.call-update) | async-done | bytes 131088 | tf_op jit(solution)/shard_map/reduce_scatter | solution.py:56
  834.0 1.7 fusion.56
  835.8 60.7 %all-gather.11.cloned.1.call-done = bf16[4096,256]{1,0:T(8,128)(2,1)} async-done(((bf16[128,256]{1,0:T(8,128)(2,1)}), bf16[4096,256]{1,0:T(8,128)(2,1)}) %all-gather.11.cloned.1.call-update) | async-done | bytes 2097168 | tf_op jit(solution)/shard_map/all_gather | solution.py:36
  896.4 2.2 gather_fusion.6
  899.2 1.7 copy.19
  900.9 1.7 pad.14
  902.6 1.2 copy.36
  904.6 1.2 reshape.165
  906.0 33.6 %all_gather.31 = bf16[1024,256]{1,0:T(8,128)(2,1)S(1)} all-gather(bf16[128,256]{1,0:T(8,128)(2,1)S(1)} %copy-done.4), channel_id=1, replica_groups=mesh['row'=32,'col'=8] {'col'}, dimensions={0}, use_global_device_ids=true | all-gather | bytes 589824 | tf_op jit(solution)/shard_map/all_gather | solution.py:39
  940.7 1.7 copy.21
  942.4 1.7 pad.15
  944.1 1.2 copy.37
  945.3 3.8 fusion.32
  949.2 4.9 reshape.168
  954.1 28.8 %reduce-scatter.21.cloned.1.call-done = f32[128,256]{1,0:T(8,128)} async-done(((f32[1024,256]{1,0:T(8,128)}), f32[128,256]{1,0:T(8,128)}) %reduce-scatter.21.cloned.1.call-update) | async-done | bytes 131088 | tf_op jit(solution)/shard_map/reduce_scatter | solution.py:62
  982.9 124.0 %reduce-scatter.23.cloned.1.call-done = f32[128,256]{1,0:T(8,128)} async-done(((f32[4096,256]{1,0:T(8,128)}), f32[128,256]{1,0:T(8,128)}) %reduce-scatter.23.cloned.1.call-update) | async-done | bytes 131088 | tf_op jit(solution)/shard_map/reduce_scatter | solution.py:56
  1106.9 1.7 multiply_subtract_fusion
  (61 shorter events, 10.0 us)
Async XLA Ops:
  6.5 72.6 %copy-start = (bf16[1,1,14,128,128]{4,3,2,1,0:T(8,128)(2,1)S(1)}, bf16[1,1,14,128,128]{4,3,2,1,0:T(8,128)(2,1)}, u32[]{:S(2)}) copy-start(bf16[1,1,14,128,128]{4,3,2,1,0:T(8,128)(2,1)} %param.10) | copy-start | bytes 1376260
  6.5 70.4 %all-gather.5.cloned.1.call-start = ((), (), s32[]{:S(2)}) async-start(), calls=%async_computation.8 | async-start | bytes 2162688 | tf_op jit(solution)/shard_map/all_gather | solution.py:36
  8.2 155.2 %reduce-scatter.9.cloned.1.call-start = ((), (), s32[]{:S(2)}) async-start(), calls=%async_computation.9 | async-start | bytes 1179648 | tf_op jit(solution)/shard_map/reduce_scatter | solution.py:62
  85.1 1.3 copy-start.3
  86.4 201.3 %reduce-scatter.11.cloned.1.call-start = ((), (), s32[]{:S(2)}) async-start(), calls=%async_computation.10 | async-start | bytes 4325376 | tf_op jit(solution)/shard_map/reduce_scatter | solution.py:56
  134.1 0.7 copy-start.8
  134.1 153.6 %copy-start.1 = (f32[128,256]{1,0:T(8,128)S(1)}, f32[128,256]{1,0:T(8,128)}, u32[]{:S(2)}) copy-start(f32[128,256]{1,0:T(8,128)} %param.9) | copy-start | bytes 393220
  134.2 215.9 %all-gather.7.cloned.1.call-start = ((), (), s32[]{:S(2)}) async-start(), calls=%async_computation.11 | async-start | bytes 2162688 | tf_op jit(solution)/shard_map/all_gather | solution.py:36
  289.3 147.3 %reduce-scatter.13.cloned.1.call-start = ((), (), s32[]{:S(2)}) async-start(), calls=%async_computation.12 | async-start | bytes 1179648 | tf_op jit(solution)/shard_map/reduce_scatter | solution.py:62
  358.3 1.3 copy-start.6
  359.6 201.1 %reduce-scatter.15.cloned.1.call-start = ((), (), s32[]{:S(2)}) async-start(), calls=%async_computation.13 | async-start | bytes 4325376 | tf_op jit(solution)/shard_map/reduce_scatter | solution.py:56
  407.4 153.3 %copy-start.2 = (f32[128,256]{1,0:T(8,128)S(1)}, f32[128,256]{1,0:T(8,128)}, u32[]{:S(2)}) copy-start(f32[128,256]{1,0:T(8,128)} %param.9) | copy-start | bytes 393220
  407.5 215.7 %all-gather.9.cloned.1.call-start = ((), (), s32[]{:S(2)}) async-start(), calls=%async_computation.14 | async-start | bytes 2162688 | tf_op jit(solution)/shard_map/all_gather | solution.py:36
  562.4 147.3 %reduce-scatter.17.cloned.1.call-start = ((), (), s32[]{:S(2)}) async-start(), calls=%async_computation.15 | async-start | bytes 1179648 | tf_op jit(solution)/shard_map/reduce_scatter | solution.py:62
  631.3 1.3 copy-start.5
  632.6 201.4 %reduce-scatter.19.cloned.1.call-start = ((), (), s32[]{:S(2)}) async-start(), calls=%async_computation.16 | async-start | bytes 4325376 | tf_op jit(solution)/shard_map/reduce_scatter | solution.py:56
  680.7 215.8 %all-gather.11.cloned.1.call-start = ((), (), s32[]{:S(2)}) async-start(), calls=%async_computation.17 | async-start | bytes 2162688 | tf_op jit(solution)/shard_map/all_gather | solution.py:36
  835.7 147.2 %reduce-scatter.21.cloned.1.call-start = ((), (), s32[]{:S(2)}) async-start(), calls=%async_computation.18 | async-start | bytes 1179648 | tf_op jit(solution)/shard_map/reduce_scatter | solution.py:62
  904.6 1.3 copy-start.4
  905.9 201.0 %reduce-scatter.23.cloned.1.call-start = ((), (), s32[]{:S(2)}) async-start(), calls=%async_computation.19 | async-start | bytes 4325376 | tf_op jit(solution)/shard_map/reduce_scatter | solution.py:56
  954.0 152.9 %copy-start.7 = (f32[128,256]{1,0:T(8,128)S(1)}, f32[128,256]{1,0:T(8,128)}, u32[]{:S(2)}) copy-start(f32[128,256]{1,0:T(8,128)} %get-tuple-element.8) | copy-start | bytes 393220
Sparse Core Ops, SparseCore 0:
  9.2 67.6 all-gather.4
  86.5 76.7 reduce-scatter.8
  166.0 121.6 reduce-scatter.10
  289.6 60.4 all-gather.6
  359.7 76.9 reduce-scatter.12
  439.0 121.6 reduce-scatter.14
  562.6 60.5 all-gather.8
  632.7 76.9 reduce-scatter.16
  712.4 121.6 reduce-scatter.18
  835.9 60.5 all-gather.10
  906.0 76.8 reduce-scatter.20
  985.3 121.6 reduce-scatter.22
where the time goes:
time: 1120 us
  waiting for transfers between devices  858 us (77%)
  blocking collectives  134 us (12%)
  local copies, waits for them, and re-layouts  74.1 us (7%)
  matrix products  22.6 us (2%)
  between operations  17.4 us (2%)
    reduce_scatter x4, waiting for transfers between devices, apply_matrix(): lax.psum_scatter(far_partial.reshape(far_count * tile_size, vec_width), '...  497 us
    all_gather x4, waiting for transfers between devices, apply_matrix(): lax.all_gather(low_vectors, 'row', axis=0, tiled=True)  250 us
    all_gather x4, blocking collectives, apply_matrix(): lax.all_gather(low_vectors, 'col', axis=0, tiled=True)  134 us
    reduce_scatter x4, waiting for transfers between devices, apply_matrix(): lax.psum_scatter(near_partial.reshape(near_count * tile_size, vec_width),...  111 us
    unnamed x34, local copies, waits for them, and re-layouts  24 us
  transfers between devices with their start and end apart: 12, of which 12 were waited for; matrix products, arithmetic and copies ran while one was open for 5% of the time, Pallas kernels for 0%

commit v1 on v0

--- a/solution.py
+++ b/solution.py
@@ -33,9 +33,9 @@
 
     def apply_matrix(vectors):
         low_vectors = vectors.astype(jnp.bfloat16)
-        far_vectors = lax.all_gather(low_vectors, "row", axis=0, tiled=True).reshape(
-            far_count, tile_size, vec_width
-        )
+        far_vectors = jnp.concatenate(
+            lax.all_to_all(jnp.stack([low_vectors] * lax.axis_size("row")), "row", 0, 0), axis=0
+        ).reshape(far_count, tile_size, vec_width)
         near_vectors = lax.all_gather(low_vectors, "col", axis=0, tiled=True).reshape(
             near_count, tile_size, vec_width
         )

time: 1120 us -> 1080 us (0.964)
  waiting for transfers between devices: 858 us -> 650 us
  blocking collectives: 134 us -> 295 us
    all_gather x4 -> x0, waiting for transfers between devices: 250 us -> none  [apply_matrix(): lax.all_gather(low_vectors, 'row', axis=0, tiled=True)]
    all_to_all x0 -> x3, blocking collectives: none -> 162 us  [apply_matrix(): lax.all_to_all(jnp.stack([low_vectors] * lax.axis_size('row')), 'row', 0, 0)]
    all_to_all x0 -> x1, waiting for transfers between devices: none -> 49.7 us  [apply_matrix(): lax.all_to_all(jnp.stack([low_vectors] * lax.axis_size('row')), 'row', 0, 0)]
    unnamed x34 -> x40, local copies, waits for them, and re-layouts: 24 us -> 24 us
  transfers between devices with their start and end apart: 12 -> 9, of which waited for: 12 -> 9; matrix products, arithmetic and copies ran while one was open for 5% -> 6% of each run, Pallas kernels for 0% -> 0%
where the time goes in v1:
time: 1080 us; the launch traced here: 1070 us
  waiting for transfers between devices  650 us (60%)
  blocking collectives  295 us (27%)
  local copies, waits for them, and re-layouts  70.9 us (7%)
  matrix products  22.4 us (2%)
  between operations  17.5 us (2%)
    reduce_scatter x4, waiting for transfers between devices, apply_matrix(): lax.psum_scatter(far_partial.reshape(far_count * tile_size, vec_width), '...  497 us
    all_to_all x3, blocking collectives, apply_matrix(): lax.all_to_all(jnp.stack([low_vectors] * lax.axis_size('row')), 'row', 0, 0)  162 us
    all_gather x4, blocking collectives, apply_matrix(): lax.all_gather(low_vectors, 'col', axis=0, tiled=True)  134 us
    reduce_scatter x4, waiting for transfers between devices, apply_matrix(): lax.psum_scatter(near_partial.reshape(near_count * tile_size, vec_width),...  103 us
    all_to_all x1, waiting for transfers between devices, apply_matrix(): lax.all_to_all(jnp.stack([low_vectors] * lax.axis_size('row')), 'row', 0, 0)  49.7 us
    unnamed x40, local copies, waits for them, and re-layouts  24 us
  transfers between devices with their start and end apart: 9, of which 9 were waited for; matrix products, arithmetic and copies ran while one was open for 6% of the time, Pallas kernels for 0%

profile of v1, /device:TPU:2, one launch (start us, length us, event | category | flops | bytes accessed | tf_op | source)
XLA Modules:
  0.0 1074.3 jit_solution(9172764070397076197)
XLA Ops:
  6.5 1.0 convert_element_type.14
  7.5 1.6 stack.8
  9.1 10.0 all-to-all-start
  19.8 49.7 %all-to-all-done = bf16[32,128,256]{2,1,0:T(8,128)(2,1)S(1)} async-done(((bf16[32,128,256]{2,1,0:T(8,128)(2,1)}), bf16[32,128,256]{2,1,0:T(8,128)(2,1)S(1)}, u32[]{:S(2)}, u32[]{:S(2)}) %all-to-all-start) | async-done | bytes 2097184 | tf_op jit(solution)/shard_map/all_to_all | solution.py:37
  70.8 1.7 copy.7
  72.5 1.7 pad.8
  74.2 1.2 copy.30
  75.5 0.8 fusion.43
  76.3 1.2 reshape.142
  77.6 33.1 %all_gather.12 = bf16[1024,256]{1,0:T(8,128)(2,1)S(1)} all-gather(bf16[128,256]{1,0:T(8,128)(2,1)S(1)} %convert_element_type.14), channel_id=1, replica_groups=mesh['row'=32,'col'=8] {'col'}, dimensions={0}, use_global_device_ids=true | all-gather | bytes 589824 | tf_op jit(solution)/shard_map/all_gather | solution.py:39
  111.8 1.7 copy.9
  113.5 1.7 pad.9
  115.2 1.2 copy.31
  116.5 3.8 fusion.35
  120.2 4.9 reshape.145
  129.7 23.5 %reduce-scatter.9.cloned.1.call-done = f32[128,256]{1,0:T(8,128)} async-done(((f32[1024,256]{1,0:T(8,128)}), f32[128,256]{1,0:T(8,128)}) %reduce-scatter.9.cloned.1.call-update) | async-done | bytes 131088 | tf_op jit(solution)/shard_map/reduce_scatter | solution.py:62
  153.2 124.4 %reduce-scatter.11.cloned.1.call-done = f32[128,256]{1,0:T(8,128)} async-done(((f32[4096,256]{1,0:T(8,128)}), f32[128,256]{1,0:T(8,128)}) %reduce-scatter.11.cloned.1.call-update) | async-done | bytes 131088 | tf_op jit(solution)/shard_map/reduce_scatter | solution.py:56
  277.6 1.7 fusion.58
  279.4 53.9 %all_to_all.20 = bf16[32,128,256]{2,1,0:T(8,128)(2,1)S(1)} all-to-all(bf16[32,128,256]{2,1,0:T(8,128)(2,1)S(1)} %stack.9), channel_id=1, replica_groups=mesh['row'=32,'col'=8] {'row'}, dimensions={0} | all-to-all | bytes 4194304 | tf_op jit(solution)/shard_map/all_to_all | solution.py:37
  334.6 1.7 copy.11
  336.3 1.7 pad.10
  338.0 1.2 copy.32
  339.2 0.8 fusion.42
  340.0 1.2 reshape.147
  341.3 33.4 %all_gather.13 = bf16[1024,256]{1,0:T(8,128)(2,1)S(1)} all-gather(bf16[128,256]{1,0:T(8,128)(2,1)S(1)} %get-tuple-element.11), channel_id=1, replica_groups=mesh['row'=32,'col'=8] {'col'}, dimensions={0}, use_global_device_ids=true | all-gather | bytes 589824 | tf_op jit(solution)/shard_map/all_gather | solution.py:39
  374.8 0.7 gather_fusion.3
  376.0 1.7 copy.13
  377.7 1.7 pad.11
  379.4 1.2 copy.33
  380.7 3.8 fusion.34
  384.4 4.9 reshape.150
  389.6 26.4 %reduce-scatter.13.cloned.1.call-done = f32[128,256]{1,0:T(8,128)} async-done(((f32[1024,256]{1,0:T(8,128)}), f32[128,256]{1,0:T(8,128)}) %reduce-scatter.13.cloned.1.call-update) | async-done | bytes 131088 | tf_op jit(solution)/shard_map/reduce_scatter | solution.py:62
  416.0 124.1 %reduce-scatter.15.cloned.1.call-done = f32[128,256]{1,0:T(8,128)} async-done(((f32[4096,256]{1,0:T(8,128)}), f32[128,256]{1,0:T(8,128)}) %reduce-scatter.15.cloned.1.call-update) | async-done | bytes 131088 | tf_op jit(solution)/shard_map/reduce_scatter | solution.py:56
  540.1 1.6 fusion.57
  542.0 53.9 %all_to_all.21 = bf16[32,128,256]{2,1,0:T(8,128)(2,1)S(1)} all-to-all(bf16[32,128,256]{2,1,0:T(8,128)(2,1)S(1)} %stack.10), channel_id=1, replica_groups=mesh['row'=32,'col'=8] {'row'}, dimensions={0} | all-to-all | bytes 4194304 | tf_op jit(solution)/shard_map/all_to_all | solution.py:37
  597.1 1.7 copy.15
  598.8 1.7 pad.12
  600.5 1.2 copy.34
  601.7 0.8 fusion.41
  602.5 1.2 reshape.152
  603.8 33.6 %all_gather.14 = bf16[1024,256]{1,0:T(8,128)(2,1)S(1)} all-gather(bf16[128,256]{1,0:T(8,128)(2,1)S(1)} %get-tuple-element.9), channel_id=1, replica_groups=mesh['row'=32,'col'=8] {'col'}, dimensions={0}, use_global_device_ids=true | all-gather | bytes 589824 | tf_op jit(solution)/shard_map/all_gather | solution.py:39
  638.7 1.7 copy.17
  640.5 1.7 pad.13
  642.2 1.2 copy.35
  643.4 3.8 fusion.33
  647.2 4.9 reshape.155
  652.2 26.5 %reduce-scatter.17.cloned.1.call-done = f32[128,256]{1,0:T(8,128)} async-done(((f32[1024,256]{1,0:T(8,128)}), f32[128,256]{1,0:T(8,128)}) %reduce-scatter.17.cloned.1.call-update) | async-done | bytes 131088 | tf_op jit(solution)/shard_map/reduce_scatter | solution.py:62
  678.8 124.2 %reduce-scatter.19.cloned.1.call-done = f32[128,256]{1,0:T(8,128)} async-done(((f32[4096,256]{1,0:T(8,128)}), f32[128,256]{1,0:T(8,128)}) %reduce-scatter.19.cloned.1.call-update) | async-done | bytes 131088 | tf_op jit(solution)/shard_map/reduce_scatter | solution.py:56
  803.0 1.7 fusion.56
  804.9 53.9 %all_to_all.22 = bf16[32,128,256]{2,1,0:T(8,128)(2,1)S(1)} all-to-all(bf16[32,128,256]{2,1,0:T(8,128)(2,1)S(1)} %stack.11), channel_id=1, replica_groups=mesh['row'=32,'col'=8] {'row'}, dimensions={0} | all-to-all | bytes 4194304 | tf_op jit(solution)/shard_map/all_to_all | solution.py:37
  860.0 1.7 copy.19
  861.7 1.7 pad.14
  863.4 1.2 copy.36
  864.6 0.8 fusion.40
  865.5 1.2 reshape.157
  866.8 33.6 %all_gather.15 = bf16[1024,256]{1,0:T(8,128)(2,1)S(1)} all-gather(bf16[128,256]{1,0:T(8,128)(2,1)S(1)} %get-tuple-element.6), channel_id=1, replica_groups=mesh['row'=32,'col'=8] {'col'}, dimensions={0}, use_global_device_ids=true | all-gather | bytes 589824 | tf_op jit(solution)/shard_map/all_gather | solution.py:39
  901.6 1.7 copy.21
  903.4 1.7 pad.15
  905.1 1.2 copy.37
  906.3 3.8 fusion.32
  910.1 4.9 reshape.160
  915.1 26.6 %reduce-scatter.21.cloned.1.call-done = f32[128,256]{1,0:T(8,128)} async-done(((f32[1024,256]{1,0:T(8,128)}), f32[128,256]{1,0:T(8,128)}) %reduce-scatter.21.cloned.1.call-update) | async-done | bytes 131088 | tf_op jit(solution)/shard_map/reduce_scatter | solution.py:62
  941.7 124.2 %reduce-scatter.23.cloned.1.call-done = f32[128,256]{1,0:T(8,128)} async-done(((f32[4096,256]{1,0:T(8,128)}), f32[128,256]{1,0:T(8,128)}) %reduce-scatter.23.cloned.1.call-update) | async-done | bytes 131088 | tf_op jit(solution)/shard_map/reduce_scatter | solution.py:56
  1065.8 1.7 multiply_subtract_fusion
  (64 shorter events, 12.1 us)
Async XLA Ops:
  6.5 63.7 %copy-start = (bf16[1,1,14,128,128]{4,3,2,1,0:T(8,128)(2,1)S(1)}, bf16[1,1,14,128,128]{4,3,2,1,0:T(8,128)(2,1)}, u32[]{:S(2)}) copy-start(bf16[1,1,14,128,128]{4,3,2,1,0:T(8,128)(2,1)} %param.10) | copy-start | bytes 1376260
  9.1 10.1 copy-start.10
  9.1 10.1 copy-start.11
  9.1 60.4 %all-to-all-start = ((bf16[32,128,256]{2,1,0:T(8,128)(2,1)}), bf16[32,128,256]{2,1,0:T(8,128)(2,1)S(1)}, u32[]{:S(2)}, u32[]{:S(2)}) async-start(bf16[32,128,256]{2,1,0:T(8,128)(2,1)} %stack.8), calls=%async_computation | async-start | bytes 4194304 | tf_op jit(solution)/shard_map/all_to_all | solution.py:37
  19.1 134.1 %reduce-scatter.9.cloned.1.call-start = ((), (), s32[]{:S(2)}) async-start(), calls=%async_computation.12 | async-start | bytes 1179648 | tf_op jit(solution)/shard_map/reduce_scatter | solution.py:62
  77.5 200.1 %reduce-scatter.11.cloned.1.call-start = ((), (), s32[]{:S(2)}) async-start(), calls=%async_computation.13 | async-start | bytes 4325376 | tf_op jit(solution)/shard_map/reduce_scatter | solution.py:56
  77.6 34.2 %copy-start.8 = (s32[1024]{0:T(1024)}, s32[1024]{0:T(1024)S(1)}, u32[]{:S(2)}) copy-start(s32[1024]{0:T(1024)S(1)} %pad_clamp_fusion) | copy-start | bytes 12292
  125.1 0.7 copy-start.9
  125.1 152.4 %copy-start.5 = (f32[128,256]{1,0:T(8,128)S(1)}, f32[128,256]{1,0:T(8,128)}, u32[]{:S(2)}) copy-start(f32[128,256]{1,0:T(8,128)} %param.9) | copy-start | bytes 393220
  125.2 290.8 %reduce-scatter.13.cloned.1.call-start = ((), (), s32[]{:S(2)}) async-start(), calls=%async_computation.14 | async-start | bytes 1179648 | tf_op jit(solution)/shard_map/reduce_scatter | solution.py:62
  341.3 198.8 %reduce-scatter.15.cloned.1.call-start = ((), (), s32[]{:S(2)}) async-start(), calls=%async_computation.15 | async-start | bytes 4325376 | tf_op jit(solution)/shard_map/reduce_scatter | solution.py:56
  389.3 150.7 %copy-start.3 = (f32[128,256]{1,0:T(8,128)S(1)}, f32[128,256]{1,0:T(8,128)}, u32[]{:S(2)}) copy-start(f32[128,256]{1,0:T(8,128)} %get-tuple-element.12) | copy-start | bytes 393220
  389.3 150.7 %copy-start.6 = (f32[128,256]{1,0:T(8,128)S(1)}, f32[128,256]{1,0:T(8,128)}, u32[]{:S(2)}) copy-start(f32[128,256]{1,0:T(8,128)} %param.9) | copy-start | bytes 393220
  389.4 289.4 %reduce-scatter.17.cloned.1.call-start = ((), (), s32[]{:S(2)}) async-start(), calls=%async_computation.16 | async-start | bytes 1179648 | tf_op jit(solution)/shard_map/reduce_scatter | solution.py:62
  603.8 199.2 %reduce-scatter.19.cloned.1.call-start = ((), (), s32[]{:S(2)}) async-start(), calls=%async_computation.17 | async-start | bytes 4325376 | tf_op jit(solution)/shard_map/reduce_scatter | solution.py:56
  652.1 150.9 %copy-start.1 = (f32[128,256]{1,0:T(8,128)S(1)}, f32[128,256]{1,0:T(8,128)}, u32[]{:S(2)}) copy-start(f32[128,256]{1,0:T(8,128)} %get-tuple-element.10) | copy-start | bytes 393220
  652.1 150.9 %copy-start.4 = (f32[128,256]{1,0:T(8,128)S(1)}, f32[128,256]{1,0:T(8,128)}, u32[]{:S(2)}) copy-start(f32[128,256]{1,0:T(8,128)} %get-tuple-element.12) | copy-start | bytes 393220
  652.1 289.6 %reduce-scatter.21.cloned.1.call-start = ((), (), s32[]{:S(2)}) async-start(), calls=%async_computation.18 | async-start | bytes 1179648 | tf_op jit(solution)/shard_map/reduce_scatter | solution.py:62
  866.7 199.1 %reduce-scatter.23.cloned.1.call-start = ((), (), s32[]{:S(2)}) async-start(), calls=%async_computation.19 | async-start | bytes 4325376 | tf_op jit(solution)/shard_map/reduce_scatter | solution.py:56
  915.0 150.9 %copy-start.2 = (f32[128,256]{1,0:T(8,128)S(1)}, f32[128,256]{1,0:T(8,128)}, u32[]{:S(2)}) copy-start(f32[128,256]{1,0:T(8,128)} %get-tuple-element.10) | copy-start | bytes 393220
  915.0 150.9 %copy-start.7 = (f32[128,256]{1,0:T(8,128)S(1)}, f32[128,256]{1,0:T(8,128)}, u32[]{:S(2)}) copy-start(f32[128,256]{1,0:T(8,128)} %get-tuple-element.8) | copy-start | bytes 393220
Sparse Core Ops, SparseCore 0:
  77.6 75.4 reduce-scatter.8
  155.9 121.6 reduce-scatter.10
  341.4 74.5 reduce-scatter.12
  418.4 121.6 reduce-scatter.14
  603.9 74.7 reduce-scatter.16
  681.3 121.6 reduce-scatter.18
  866.8 74.7 reduce-scatter.20
  944.2 121.6 reduce-scatter.22
